TPU v7x, 32 devices: a whole 2x2x4 slice. The times are simulated.
32 devices in a mesh: ctx: 8 (over z, core), tp: 4 (over y, x).
Axes of the slice: x: 2, y: 2, z: 4, core: 2. Of those that a mesh axis runs over, the one named last changes fastest.
Arguments:
- queries: bfloat16 [1024, 8192], P('ctx', 'tp'), may hold values from -6 to 6
- keys_in: bfloat16 [1024, 8192], P('ctx', 'tp'), may hold values from -6 to 6
- values_in: bfloat16 [1024, 8192], P('ctx', 'tp'), may hold values from -6 to 6
- decay_rates: float32 [8192, 16], P('tp'), may hold values from 0.00029296876 to 0.03
- residues: float32 [8192, 16], P('tp'), may hold values from -1.5 to 1.5
- skip_gain: float32 [8192], P('tp'), may hold values from -4 to 4
- cotangent: bfloat16 [1024, 8192], P('ctx', 'tp'), may hold values from -6 to 6
Outputs:
- operator_out: bfloat16 [1024, 8192], P('ctx', 'tp')
- grad_queries: bfloat16 [1024, 8192], P('ctx', 'tp')
- grad_keys: bfloat16 [1024, 8192], P('ctx', 'tp')
- grad_values: bfloat16 [1024, 8192], P('ctx', 'tp')
- grad_residues: float32 [8192, 16], P('tp')
All inputs are finite; a program needn't handle non-finite values.
Results may differ from a plain program's by a relative error of at most 0.0054.
Values may be sent and summed in bfloat16 or wider, within the bound.
No kernel may reach another device: no remote copies, remote signals or barrier semaphores. Data moves between devices by JAX's collectives and lax.ppermute only.
A program may use at most 64 MiB of HBM per device.

v0:
```python
from functools import partial
import math

import jax
import jax.numpy as jnp
from jax import lax
from jax.experimental import pallas as pl
from jax.experimental.pallas import tpu as pltpu
from jax.sharding import PartitionSpec as P

F32 = jnp.float32
WIRE = jnp.bfloat16
LANES = 128
UNROLL = 8
STEP_ROWS = 32
KERNEL = pltpu.CompilerParams(vmem_limit_bytes=24 * 1024 * 1024)
HBM = pl.BlockSpec(memory_space=pltpu.HBM)
VMEM = pl.BlockSpec(memory_space=pltpu.VMEM)


def reorder(rows, inner, transpose):
    outer = rows // inner
    to = lax.broadcasted_iota(jnp.int32, (rows, rows), 0)
    fro = lax.broadcasted_iota(jnp.int32, (rows, rows), 1)
    if transpose:
        to, fro = fro, to
    same = (to % outer == fro // inner) & (to // outer == fro % inner)
    return jnp.where(same, 1.0, 0.0).astype(jnp.bfloat16)


def tree_sum(items):
    items = list(items)
    while len(items) > 1:
        items = [
            items[i] + items[i + 1] if i + 1 < len(items) else items[i]
            for i in range(0, len(items), 2)
        ]
    return items[0]


def states_kernel(
    q_hbm,
    k_hbm,
    v_hbm,
    ct_hbm,
    rate_hbm,
    res_hbm,
    keep_ref,
    send_ref,
    q_ref,
    k_ref,
    v_ref,
    ct_ref,
    gated_ref,
    pulled_ref,
    rate_ref,
    coef_ref,
    rate_cols,
    res_cols,
    states,
    sems,
):
    seq, channels = q_ref.shape
    modes = rate_cols.shape[0]
    blocks = gated_ref.shape[0]
    sub = channels // (blocks * LANES)
    part = math.gcd(seq, STEP_ROWS)
    parts = seq // part
    tables = [
        pltpu.make_async_copy(rate_hbm, rate_cols, sems.at[4 * parts]),
        pltpu.make_async_copy(res_hbm, res_cols, sems.at[4 * parts + 1]),
    ]
    lines = []
    for i in range(parts):
        rows = pl.ds(i * part, part)
        pairs = ((k_hbm, k_ref), (v_hbm, v_ref), (ct_hbm, ct_ref), (q_hbm, q_ref))
        for j, (source, target) in enumerate(pairs):
            lines.append(
                pltpu.make_async_copy(source.at[rows], target.at[rows], sems.at[4 * i + j])
            )
    for copy in tables + lines:
        copy.start()
    for copy in tables:
        copy.wait()
    for b in range(blocks):
        for s in range(sub):
            cols = slice((b * sub + s) * LANES, (b * sub + s + 1) * LANES)
            rows = pl.ds(b * modes * sub + s, modes, stride=sub)
            rate_ref[rows, :] = rate_cols[:, cols]
            coef_ref[rows, :] = res_cols[:, cols]
    rate = rate_ref[...]
    coef_ref[...] = coef_ref[...] * jnp.sqrt(1.0 - jnp.exp(-2.0 * rate))
    to_scan = reorder(part * sub, part, False)

    def to_scan_order(left, right, i, target):
        rows = slice(i * part, (i + 1) * part)
        product = (left[rows, :].astype(F32) * right[rows, :].astype(F32)).astype(jnp.bfloat16)
        stacked = jnp.concatenate(
            [
                jnp.concatenate(
                    [
                        product[:, (b * sub + s) * LANES : (b * sub + s + 1) * LANES]
                        for s in range(sub)
                    ],
                    axis=0,
                )
                for b in range(blocks)
            ],
            axis=1,
        )
        ordered = jnp.dot(to_scan, stacked, preferred_element_type=F32)
        for b in range(blocks):
            target[b, i * part * sub : (i + 1) * part * sub, :] = ordered[
                :, b * LANES : (b + 1) * LANES
            ]

    mode_rows_of = partial(mode_rows, modes=modes, sub=sub)
    for i in range(parts):
        for copy in lines[4 * i : 4 * i + 4]:
            copy.wait()
        to_scan_order(k_ref, v_ref, i, gated_ref)
        to_scan_order(ct_ref, q_ref, i, pulled_ref)
        for b in range(blocks):
            decay = [jnp.exp(-rate_ref[r, :]) for r in mode_rows_of(b)]

            def forward(j, carry):
                held, inner = list(carry[0]), list(carry[1])
                for u in range(UNROLL):
                    at = pl.ds(pl.multiple_of((i * part + j * UNROLL + u) * sub, sub), sub)
                    x = gated_ref[b, at, :]
                    p = pulled_ref[b, at, :]
                    for n in range(modes):
                        held[n] = decay[n] * held[n] + x
                        inner[n] = inner[n] + p * held[n]
                return tuple(held), tuple(inner)

            if i == 0:
                first = tuple(jnp.zeros((sub, LANES), F32) for _ in range(modes))
                carry = (first, first)
            else:
                carry = tuple(tuple(states[kind, r, :] for r in mode_rows_of(b)) for kind in (0, 2))
            ends, inner = lax.fori_loop(0, part // UNROLL, forward, carry)
            for n, r in enumerate(mode_rows_of(b)):
                states[0, r, :] = ends[n]
                states[2, r, :] = inner[n]

    for b in range(blocks):
        decay = [jnp.exp(-rate_ref[r, :]) for r in mode_rows_of(b)]

        def backward(j, carry):
            held = list(carry)
            for u in range(UNROLL):
                at = pl.ds(pl.multiple_of((seq - 1 - (j * UNROLL + u)) * sub, sub), sub)
                p = pulled_ref[b, at, :]
                for n in range(modes):
                    held[n] = decay[n] * held[n] + p
            return tuple(held)

        first = tuple(jnp.zeros((sub, LANES), F32) for _ in range(modes))
        starts = lax.fori_loop(0, seq // UNROLL, backward, first)
        for n, r in enumerate(mode_rows_of(b)):
            states[1, r, :] = starts[n]

    half = keep_ref.shape[1]
    core = lax.axis_index("ctx") % 2
    keep_ref[...] = states[:, pl.ds(pl.multiple_of(core * half, half), half), :]
    send_ref[...] = states[:, pl.ds(pl.multiple_of((1 - core) * half, half), half), :]


def own_rows(rate_ref, half):
    core = lax.axis_index("ctx") % 2
    return rate_ref[pl.ds(pl.multiple_of(core * half, half), half), :]


def joined(is_right, mine, other, span, step):
    left = [jnp.where(is_right, o, m) for m, o in zip(mine, other)]
    right = [jnp.where(is_right, m, o) for m, o in zip(mine, other)]
    return (
        span * left[0] + right[0],
        left[1] + span * right[1],
        left[2] + right[2] + step * right[1] * left[0],
    )


def put_wire(wire_ref, is_last, next_right, block):
    if is_last:
        wire_ref[0] = jnp.where(next_right, block[1], block[0]).astype(wire_ref.dtype)
        wire_ref[1] = block[2].astype(wire_ref.dtype)
    else:
        for kind in range(3):
            wire_ref[kind] = block[kind].astype(wire_ref.dtype)


def pair_kernel(seq, is_last, keep_ref, got_ref, rate_ref, after_ref, block_ref, wire_ref):
    rate = own_rows(rate_ref, keep_ref.shape[1])
    place = lax.axis_index("ctx")
    block = joined(
        place % 2 == 1,
        [keep_ref[i] for i in range(3)],
        [got_ref[i] for i in range(3)],
        jnp.exp(-rate * seq),
        jnp.exp(-rate),
    )
    for kind in range(3):
        block_ref[kind] = block[kind]
    block_ref[3] = jnp.zeros_like(rate)
    block_ref[4] = jnp.zeros_like(rate)
    put_wire(wire_ref, is_last, (place // 2) % 2 == 1, block)


def carries_with(block_ref, end_state, start_state, level, seq, rate):
    place = lax.axis_index("ctx")
    is_right = (place >> level) % 2 == 1
    chips = 1 << (level - 1)
    at = (place // 2) % chips
    before = at * (2 * seq)
    behind = (chips - 1 - at) * (2 * seq)
    ahead = block_ref[3] + jnp.where(
        is_right, jnp.exp(-rate * before.astype(F32)) * end_state, 0.0
    )
    after = block_ref[4] + jnp.where(
        is_right, 0.0, jnp.exp(-rate * behind.astype(F32)) * start_state
    )
    return is_right, ahead, after


def level_kernel(
    seq, level, is_last, block_ref, got_ref, rate_ref, after_ref, out_ref, wire_ref
):
    rate = own_rows(rate_ref, block_ref.shape[1])
    got = [got_ref[i].astype(F32) for i in range(3)]
    is_right, ahead, after = carries_with(block_ref, got[0], got[1], level, seq, rate)
    block = joined(
        is_right,
        [block_ref[i] for i in range(3)],
        got,
        jnp.exp(-rate * (seq << level)),
        jnp.exp(-rate),
    )
    for kind in range(3):
        out_ref[kind] = block[kind]
    out_ref[3] = ahead
    out_ref[4] = after
    next_right = (lax.axis_index("ctx") >> (level + 1)) % 2 == 1
    put_wire(wire_ref, is_last, next_right, block)


def last_kernel(
    seq,
    level,
    block_ref,
    got_ref,
    rate_ref,
    keep_ref,
    sibling_ref,
    after_ref,
    mine_ref,
    other_ref,
):
    half = block_ref.shape[1]
    rate = own_rows(rate_ref, half)
    edge, inner = got_ref[0].astype(F32), got_ref[1].astype(F32)
    is_right, ahead, after = carries_with(block_ref, edge, edge, level, seq, rate)
    own_edge = jnp.where(is_right, block_ref[1], block_ref[0])
    total = block_ref[2] + inner + jnp.exp(-rate) * own_edge * edge
    raw = jnp.sqrt(1.0 - jnp.exp(-2.0 * rate)) * total
    core = lax.axis_index("ctx") % 2
    first = core == 0
    span = jnp.exp(-rate * seq)
    end_first = jnp.where(first, keep_ref[0], sibling_ref[0])
    start_second = jnp.where(first, sibling_ref[1], keep_ref[1])
    ahead_second = span * ahead + end_first
    after_first = span * after + start_second
    mine_ref[0:half, :] = jnp.where(first, ahead, ahead_second)
    mine_ref[half : 2 * half, :] = jnp.where(first, after_first, after)
    other_ref[0:half, :] = jnp.where(first, ahead_second, ahead)
    other_ref[half : 2 * half, :] = jnp.where(first, after, after_first)
    squares = raw * raw
    share = tree_sum([squares[i : i + 8, :] for i in range(0, half, 8)])
    for ref in (mine_ref, other_ref):
        ref[2 * half : 3 * half, :] = raw
        ref[3 * half : 3 * half + 8, :] = share


def place_halves(mine_ref, other_ref, first, target):
    half = target.shape[0] // 2
    core = lax.axis_index("ctx") % 2
    for ref, at in ((mine_ref, core), (other_ref, 1 - core)):
        rows = pl.ds(pl.multiple_of(at * half, half), half)
        target[rows, :] = ref[first : first + half, :]


def mode_rows(block, modes, sub):
    return [slice((block * modes + n) * sub, (block * modes + n + 1) * sub) for n in range(modes)]


def local_kernel(reverse, which, modes, lines_ref, rate_ref, coef_ref, after_ref, *out_refs):
    sub = rate_ref.shape[0] // (lines_ref.shape[0] * modes)
    seq = lines_ref.shape[1] // sub
    for b, out_ref in zip(which, out_refs):
        rows = mode_rows(b, modes, sub)
        decay = [jnp.exp(-rate_ref[r, :]) for r in rows]
        coef = [coef_ref[r, :] for r in rows]

        def body(j, carry):
            held = list(carry)
            for u in range(UNROLL):
                t = j * UNROLL + u
                if reverse:
                    t = seq - 1 - t
                at = pl.ds(pl.multiple_of(t * sub, sub), sub)
                x = lines_ref[b, at, :]
                total = [None] * 4
                for n in range(modes):
                    held[n] = decay[n] * held[n] + x
                    term = coef[n] * held[n]
                    total[n % 4] = term if n < 4 else total[n % 4] + term
                out_ref[at, :] = tree_sum(total)
            return tuple(held)

        first = tuple(jnp.zeros((sub, LANES), F32) for _ in range(modes))
        lax.fori_loop(0, seq // UNROLL, body, first)


def add_carries(reverse, modes, rate_ref, coef_ref, states, local_refs, target):
    sub = rate_ref.shape[0] // (len(local_refs) * modes)
    seq = local_refs[0].shape[0] // sub
    for b, local_ref in enumerate(local_refs):
        rows = mode_rows(b, modes, sub)
        decay = [jnp.exp(-rate_ref[r, :]) for r in rows]
        first = tuple(coef_ref[r, :] * states[r, :] for r in rows)

        def body(j, carry):
            held = list(carry)
            for u in range(UNROLL):
                t = j * UNROLL + u
                if reverse:
                    t = seq - 1 - t
                at = pl.ds(pl.multiple_of(t * sub, sub), sub)
                total = [local_ref[at, :], None, None, None]
                for n in range(modes):
                    held[n] = decay[n] * held[n]
                    total[n % 4] = held[n] if total[n % 4] is None else total[n % 4] + held[n]
                target[b, at, :] = tree_sum(total)
            return tuple(held)

        lax.fori_loop(0, seq // UNROLL, body, first)


def line_outputs(left, right, scales, skip_ref, scanned, targets, done_with):
    seq, channels = left.shape
    blocks = scanned.shape[0]
    sub = channels // (blocks * LANES)
    part = math.gcd(seq, STEP_ROWS)
    from_scan = reorder(part * sub, part, True)
    for i in range(seq // part):
        rows = slice(i * part, (i + 1) * part)
        stacked = jnp.concatenate(
            [scanned[b, i * part * sub : (i + 1) * part * sub, :] for b in range(blocks)], axis=1
        ).astype(jnp.bfloat16)
        ordered = jnp.dot(from_scan, stacked, preferred_element_type=F32)
        for b in range(blocks):
            for s in range(sub):
                cols = slice((b * sub + s) * LANES, (b * sub + s + 1) * LANES)
                own = ordered[s * part : (s + 1) * part, b * LANES : (b + 1) * LANES]
                line = left[rows, cols].astype(F32) * right[rows, cols].astype(F32)
                mixed = own + skip_ref[:, cols] * line.astype(jnp.bfloat16).astype(F32)
                for scale, target in zip(scales, targets):
                    target[rows, cols] = (scale[rows, cols].astype(F32) * mixed).astype(
                        jnp.bfloat16
                    )
        done_with(i, pl.ds(i * part, part))


def forward_kernel(modes, blocks, *refs):
    q_ref, k_ref, v_ref, ct_ref, rate_ref, coef_ref, skip_ref, mine_ref, other_ref, _ = refs[:10]
    local_refs = refs[10 : 10 + blocks]
    out_ref, gq_ref, token_ref, scanned, states = refs[10 + blocks :]
    token_ref[...] = jnp.zeros_like(token_ref)
    place_halves(mine_ref, other_ref, 0, states)
    add_carries(False, modes, rate_ref, coef_ref, states, local_refs, scanned)
    line_outputs(
        k_ref,
        v_ref,
        (q_ref, ct_ref),
        skip_ref,
        scanned,
        (out_ref, gq_ref),
        lambda i, at: None,
    )


def adjoint_kernel(modes, blocks, *refs):
    rate_ref, coef_ref, mine_ref, other_ref, _ = refs[:5]
    local_refs = refs[5 : 5 + blocks]
    scanned, states = refs[5 + blocks :]
    place_halves(mine_ref, other_ref, states.shape[0] // 2, states)
    add_carries(True, modes, rate_ref, coef_ref, states, local_refs, scanned)


def backward_kernel(
    q_ref,
    k_ref,
    v_ref,
    ct_ref,
    scanned,
    skip_ref,
    out_rows,
    gq_rows,
    raw_cols,
    out_hbm,
    gq_hbm,
    raw_hbm,
    gk_hbm,
    gv_hbm,
    gk_rows,
    gv_rows,
    sems,
):
    copies = []

    def start(source, target):
        copy = pltpu.make_async_copy(source, target, sems.at[len(copies)])
        copy.start()
        copies.append(copy)

    def send(i, at):
        for source, target in ((gk_rows, gk_hbm), (gv_rows, gv_hbm)):
            start(source.at[at], target.at[at])

    for source, target in ((out_rows, out_hbm), (gq_rows, gq_hbm), (raw_cols, raw_hbm)):
        start(source, target)
    line_outputs(ct_ref, q_ref, (v_ref, k_ref), skip_ref, scanned, (gk_rows, gv_rows), send)
    for copy in copies:
        copy.wait()


def add_kernel(left_ref, right_ref, after_ref, out_ref):
    out_ref[...] = left_ref[...] + right_ref[...]


def clip_kernel(limit, blocks, mine_ref, other_ref, *refs):
    share_refs, (out_ref, states) = refs[1:-2], refs[-2:]
    modes = out_ref.shape[0]
    sub = out_ref.shape[1] // (blocks * LANES)
    half = states.shape[0] // 2
    place_halves(mine_ref, other_ref, 2 * half, states)
    square = jnp.sum(tree_sum([ref[...] for ref in share_refs]))
    factor = jnp.minimum(1.0, limit * lax.rsqrt(jnp.full((1, LANES), square + 1e-06, F32)))
    for b in range(blocks):
        for s in range(sub):
            cols = slice((b * sub + s) * LANES, (b * sub + s + 1) * LANES)
            rows = pl.ds(b * modes * sub + s, modes, stride=sub)
            out_ref[:, cols] = states[rows, :] * factor


def shards(queries, keys_in, values_in, decay_rates, residues, skip_gain, cotangent):
    seq, channels = queries.shape
    modes = decay_rates.shape[1]
    ctx = lax.axis_size("ctx")
    tp = lax.axis_size("tp")
    levels = ctx.bit_length() - 1
    groups = channels // LANES
    sub = math.gcd(groups, 8)
    blocks = groups // sub
    half = modes * groups // 2
    parts = seq // math.gcd(seq, STEP_ROWS)

    def swap(value, bit):
        return lax.ppermute(value, "ctx", [(i, i ^ (1 << bit)) for i in range(ctx)])

    def rows(*shape, dtype=F32):
        return jax.ShapeDtypeStruct((*shape, LANES), dtype)

    line_shape = jax.ShapeDtypeStruct((seq, channels), jnp.bfloat16)
    table_shape = jax.ShapeDtypeStruct((modes, channels), F32)
    line_scratch = pltpu.VMEM((seq, channels), jnp.bfloat16)
    table_scratch = pltpu.VMEM((modes, channels), F32)
    elements = seq * channels * modes
    sources = (queries, keys_in, values_in, cotangent, decay_rates.T, residues.T)

    keep, send, q, k, v, ct, gated, pulled, row_rates, row_coefs = pl.pallas_call(
        states_kernel,
        in_specs=[HBM] * 6,
        out_specs=[VMEM] * 10,
        out_shape=[rows(3, half)] * 2
        + [line_shape] * 4
        + [rows(blocks, seq * sub)] * 2
        + [rows(2 * half)] * 2,
        scratch_shapes=[
            table_scratch,
            table_scratch,
            pltpu.VMEM((3, 2 * half, LANES), F32),
            pltpu.SemaphoreType.DMA((4 * parts + 2,)),
        ],
        compiler_params=KERNEL,
        cost_estimate=pl.CostEstimate(
            flops=6 * elements, bytes_accessed=8 * seq * channels, transcendentals=0
        ),
        name="chunk_states",
    )(*[pltpu.with_memory_space_constraint(item, pltpu.HBM) for item in sources])
    sibling = swap(send, 0)

    def wire(level):
        return rows(2 if level == levels - 1 else 3, half, dtype=WIRE)

    whole = rows(blocks, seq * sub)
    whole_scratch = pltpu.VMEM((blocks, seq * sub, LANES), F32)
    states_scratch = pltpu.VMEM((2 * half, LANES), F32)
    every = tuple(range(blocks))

    def local(reverse, which, after, name):
        lines = pulled if reverse else gated
        return pl.pallas_call(
            partial(local_kernel, reverse, which, modes),
            out_shape=[rows(seq * sub)] * len(which),
            compiler_params=KERNEL,
            cost_estimate=pl.CostEstimate(
                flops=4 * elements, bytes_accessed=8 * seq * channels, transcendentals=0
            ),
            name=name,
        )(lines, row_rates, row_coefs, after[:8])

    block, packed = pl.pallas_call(
        partial(pair_kernel, seq, levels == 2),
        out_shape=[rows(5, half), wire(1)],
        compiler_params=KERNEL,
        name="chip_states",
    )(keep, sibling, row_rates, row_rates[:8])
    got = swap(packed, 1)
    conv = local(False, every, block[4], "local_conv")
    for level in range(1, levels - 1):
        block, packed = pl.pallas_call(
            partial(level_kernel, seq, level, level + 1 == levels - 1),
            out_shape=[rows(5, half), wire(level + 1)],
            compiler_params=KERNEL,
            name="block_states",
        )(block, got, row_rates, conv[0])
        got = swap(packed, level + 1)
    early = every[: (blocks + 1) // 2]
    adj = local(True, early, block[4], "local_adjoint")
    mine, other = pl.pallas_call(
        partial(last_kernel, seq, levels - 1),
        out_shape=[rows(3 * half + 8)] * 2,
        compiler_params=KERNEL,
        name="carries",
    )(block, got, row_rates, keep, sibling, adj[0])
    other = swap(other, 0)
    after = mine
    if len(early) < blocks:
        adj += local(True, every[len(early) :], mine, "late_adjoint")
        after = adj[-1]

    def plus(left, right, after):
        return pl.pallas_call(
            add_kernel,
            in_specs=[VMEM] * 3,
            out_shape=rows(8),
            compiler_params=KERNEL,
            name="square_sum",
        )(left, right, after)

    def tp_swap(value, bit):
        return lax.ppermute(value, "tp", [(i, i ^ (1 << bit)) for i in range(tp)])

    square = plus(mine[3 * half :], other[3 * half :], after)
    bits = tp.bit_length() - 1
    share = tp_swap(square, 0) if bits else jnp.zeros_like(square)
    skip = skip_gain.reshape(1, channels)
    forward_out, forward_grad, after = pl.pallas_call(
        partial(forward_kernel, modes, blocks),
        out_shape=[line_shape] * 2 + [rows(8)],
        scratch_shapes=[whole_scratch, states_scratch],
        compiler_params=KERNEL,
        cost_estimate=pl.CostEstimate(
            flops=2 * elements, bytes_accessed=16 * seq * channels, transcendentals=0
        ),
        name="forward_outputs",
    )(q, k, v, ct, row_rates, row_coefs, skip, mine, other, square, *conv)
    for bit in range(1, bits):
        square = plus(square, share, after)
        share = tp_swap(square, bit)
        after = square
    scanned = pl.pallas_call(
        partial(adjoint_kernel, modes, blocks),
        out_shape=whole,
        scratch_shapes=[states_scratch],
        compiler_params=KERNEL,
        cost_estimate=pl.CostEstimate(
            flops=2 * elements, bytes_accessed=8 * seq * channels, transcendentals=0
        ),
        name="adjoint_carries",
    )(row_rates, row_coefs, mine, other, after, *adj)
    clipped = pl.pallas_call(
        partial(clip_kernel, math.sqrt(channels * tp * modes), blocks),
        out_shape=table_shape,
        scratch_shapes=[states_scratch],
        compiler_params=KERNEL,
        name="clip",
    )(mine, other, scanned, square, share)
    operator_out, grad_queries, grad_residues, grad_keys, grad_values = pl.pallas_call(
        backward_kernel,
        in_specs=[VMEM] * 9,
        out_specs=[HBM] * 5,
        out_shape=[line_shape] * 2 + [table_shape] + [line_shape] * 2,
        scratch_shapes=[line_scratch] * 2 + [pltpu.SemaphoreType.DMA((2 * parts + 3,))],
        compiler_params=KERNEL,
        cost_estimate=pl.CostEstimate(
            flops=elements, bytes_accessed=8 * seq * channels, transcendentals=0
        ),
        name="backward_outputs",
    )(q, k, v, ct, scanned, skip, forward_out, forward_grad, clipped)
    return (operator_out, grad_queries, grad_keys, grad_values, grad_residues.T)


def solution(mesh):
    lines, tables = P("ctx", "tp"), P("tp", None)
    in_specs = (lines, lines, lines, tables, tables, P("tp"), lines)
    out_specs = (lines, lines, lines, lines, tables)
    return jax.shard_map(shards, mesh=mesh, in_specs=in_specs, out_specs=out_specs, check_vma=False)
```

profile of v0, /device:TPU:0, one launch (start us, length us, event | category | flops | bytes accessed | tf_op | source)
XLA Modules:
  0.0 30.9 jit_solution(2166934434279899391)
XLA Ops:
  0.6 6.4 %chunk_states.1 = (f32[3,128,128]{2,1,0:T(8,128)S(1)}, f32[3,128,128]{2,1,0:T(8,128)S(1)}, bf16[128,2048]{1,0:T(8,128)(2,1)S(1)}, bf16[128,2048]{1,0:T(8,128)(2,...) custom-call(bf16[128,2048]{1,0:T(8,128)(2,1)} %q_hbm.1, ...), custom_call_target="tpu_custom_call" | custom-call | flops 25165824 | bytes 2097152 | tf_op jit(solution)/shard_map/chunk_states/pallas_call | solution.py:482
  7.0 0.5 %collective-permute-start = (f32[3,128,128]{2,1,0:T(8,128)S(1)}, f32[3,128,128]{2,1,0:T(8,128)S(1)}, u32[]{:S(2)}, u32[]{:S(2)}) collective-permute-start(f32[3,128,128]{2,1,0:T(8,128)S(1)} %get-tuple-element.38), channel_id=1, source_target_pairs={{0,4},{4,0},{8,12},{12,8},{16,20},{20,16},{24,28},{28,24},{1,5},{5... | collective-permute-start | bytes 589832 | tf_op jit(solution)/shard_map/ppermute | solution.py:470
  7.5 1.1 %collective-permute-done.got_ref.sibling_ref = f32[3,128,128]{2,1,0:T(8,128)S(1)} collective-permute-done((f32[3,128,128]{2,1,0:T(8,128)S(1)}, f32[3,128,128]{2,1,0:T(8,128)S(1)}, u32[]{:S(2)}, u32[]{:S(2)}) %collective-permute-start) | collective-permute-done | bytes 196640 | tf_op jit(solution)/shard_map/ppermute | solution.py:470
  8.6 0.1 chip_states.1
  8.7 3.0 %collective-permute-start.1 = (bf16[3,128,128]{2,1,0:T(8,128)(2,1)S(1)}, bf16[3,128,128]{2,1,0:T(8,128)(2,1)S(1)}, u32[]{:S(2)}, u32[]{:S(2)}) collective-permute-start(bf16[3,128,128]{2,1,0:T(8,128)(2,1)S(1)} %get-tuple-element.40), channel_id=1, source_target_pairs={{0,8},{4,12},{8,0},{12,4},{16,24},{20,28},{24,16},{28,20},{1,9},{5... | collective-permute-start | bytes 294920 | tf_op jit(solution)/shard_map/ppermute | solution.py:470
  11.7 2.3 %local_conv.1 = (f32[1024,128]{1,0:T(8,128)S(1)}, f32[1024,128]{1,0:T(8,128)S(1)}) custom-call(f32[2,1024,128]{2,1,0:T(8,128)S(1)} %get-tuple-element.41.lines_ref, f32[256,128]{1,0:T(8,128)S(1)} %get-tuple-element.35.rate_ref.refs_4_.refs_0_, f32[256,128]{1,0:T(8,128)S(1)} %get-tuple-element.36.coef_ref.refs_5_.refs_1_, ...), custom_call_target="tpu_custom_call" | custom-call | flops 16777216 | bytes 2097152 | tf_op jit(solution)/shard_map/local_conv/pallas_call | solution.py:514
  14.0 0.8 %collective-permute-done.1.got_ref = bf16[3,128,128]{2,1,0:T(8,128)(2,1)S(1)} collective-permute-done((bf16[3,128,128]{2,1,0:T(8,128)(2,1)S(1)}, bf16[3,128,128]{2,1,0:T(8,128)(2,1)S(1)}, u32[]{:S(2)}, u32[]{:S(2)}) %collective-permute-start.1) | collective-permute-done | bytes 98336 | tf_op jit(solution)/shard_map/ppermute | solution.py:470
  14.8 0.1 block_states.1
  14.9 2.8 %collective-permute-start.2 = (bf16[2,128,128]{2,1,0:T(8,128)(2,1)S(1)}, bf16[2,128,128]{2,1,0:T(8,128)(2,1)S(1)}, u32[]{:S(2)}, u32[]{:S(2)}) collective-permute-start(bf16[2,128,128]{2,1,0:T(8,128)(2,1)S(1)} %get-tuple-element.44), channel_id=1, source_target_pairs={{0,16},{4,20},{8,24},{12,28},{16,0},{20,4},{24,8},{28,12},{1,17},{... | collective-permute-start | bytes 196616 | tf_op jit(solution)/shard_map/ppermute | solution.py:470
  17.7 1.2 %local_adjoint.1.after_ref.refs_5_ = f32[1024,128]{1,0:T(8,128)S(1)} custom-call(f32[2,1024,128]{2,1,0:T(8,128)S(1)} %get-tuple-element.45.lines_ref, f32[256,128]{1,0:T(8,128)S(1)} %get-tuple-element.35.rate_ref.refs_4_.refs_0_, f32[256,128]{1,0:T(8,128)S(1)} %get-tuple-element.36.coef_ref.refs_5_.refs_1_, f32[8,128]{1,0:T(8,128)S(1)} %slice_bitcast_fusion.after_ref), custom_call_target="tpu_custom_call" | custom-call | flops 16777216 | bytes 2097152 | tf_op jit(solution)/shard_map/local_adjoint/pallas_call | solution.py:514
  18.9 1.5 %collective-permute-done.2.got_ref = bf16[2,128,128]{2,1,0:T(8,128)(2,1)S(1)} collective-permute-done((bf16[2,128,128]{2,1,0:T(8,128)(2,1)S(1)}, bf16[2,128,128]{2,1,0:T(8,128)(2,1)S(1)}, u32[]{:S(2)}, u32[]{:S(2)}) %collective-permute-start.2) | collective-permute-done | bytes 65568 | tf_op jit(solution)/shard_map/ppermute | solution.py:470
  20.3 0.1 carries.1
  20.5 0.1 collective-permute-start.3
  20.6 1.2 %late_adjoint.1.after_ref.refs_6_ = f32[1024,128]{1,0:T(8,128)S(1)} custom-call(f32[2,1024,128]{2,1,0:T(8,128)S(1)} %get-tuple-element.45.lines_ref, f32[256,128]{1,0:T(8,128)S(1)} %get-tuple-element.35.rate_ref.refs_4_.refs_0_, f32[256,128]{1,0:T(8,128)S(1)} %get-tuple-element.36.coef_ref.refs_5_.refs_1_, f32[8,128]{1,0:T(8,128)S(1)} %get-tuple-element.57.after_ref), custom_call_target="tpu_custom_call" | custom-call | flops 16777216 | bytes 2097152 | tf_op jit(solution)/shard_map/late_adjoint/pallas_call | solution.py:514
  21.8 0.2 collective-permute-done.3.refs_8_.refs_3_.other_ref
  22.0 1.6 %collective-permute-start.4 = (f32[8,128]{1,0:T(8,128)S(1)}, f32[8,128]{1,0:T(8,128)S(1)}, u32[]{:S(2)}, u32[]{:S(2)}) collective-permute-start(f32[8,128]{1,0:T(8,128)S(1)} %square_sum.2.refs_9_.left_ref), channel_id=1, source_target_pairs={{0,1},{1,0},{2,3},{3,2},{4,5},{5,4},{6,7},{7,6},{8,9},{9,8},{10,11... | collective-permute-start | bytes 12296 | tf_op jit(solution)/shard_map/ppermute | solution.py:564
  23.6 0.0 copy-done
  23.6 1.8 %forward_outputs.1 = (bf16[128,2048]{1,0:T(8,128)(2,1)S(1)}, bf16[128,2048]{1,0:T(8,128)(2,1)S(1)}, f32[8,128]{1,0:T(8,128)S(1)}) custom-call(bf16[128,2048]{1,0:T(8,128)(2,1)S(1)} %get-tuple-element.31.refs_0_.q_ref, bf16[128,2048]{1,0:T(8,128)(2,1)S(1)} %get-tuple-element.32.refs_1_.k_ref, bf16[128,2048]{1,0:T(8,128)(2,1)S(1)} %get-tuple-element.33.refs_2_.v_ref, ...), custom_call_target="tpu_custom_call" | custom-call | flops 8388608 | bytes 4194304 | tf_op jit(solution)/shard_map/forward_outputs/pallas_call | solution.py:570
  25.4 0.3 collective-permute-done.4.right_ref
  25.7 1.5 %collective-permute-start.5 = (f32[8,128]{1,0:T(8,128)S(1)}, f32[8,128]{1,0:T(8,128)S(1)}, u32[]{:S(2)}, u32[]{:S(2)}) collective-permute-start(f32[8,128]{1,0:T(8,128)S(1)} %square_sum.3.refs_4_.refs_1_), channel_id=1, source_target_pairs={{0,2},{1,3},{2,0},{3,1},{4,6},{5,7},{6,4},{7,5},{8,10},{9,11},{10,... | collective-permute-start | bytes 12296 | tf_op jit(solution)/shard_map/ppermute | solution.py:564
  27.2 1.3 %adjoint_carries.1.refs_0_.scanned = f32[2,1024,128]{2,1,0:T(8,128)S(1)} custom-call(f32[256,128]{1,0:T(8,128)S(1)} %get-tuple-element.35.rate_ref.refs_4_.refs_0_, f32[256,128]{1,0:T(8,128)S(1)} %get-tuple-element.36.coef_ref.refs_5_.refs_1_, f32[392,128]{1,0:T(8,128)S(1)} %get-tuple-element.46.refs_7_.refs_2_.mine_ref, ...), custom_call_target="tpu_custom_call" | custom-call | flops 8388608 | bytes 2097152 | tf_op jit(solution)/shard_map/adjoint_carries/pallas_call | solution.py:584
  28.5 0.8 %collective-permute-done.5.refs_2_ = f32[8,128]{1,0:T(8,128)S(1)} collective-permute-done((f32[8,128]{1,0:T(8,128)S(1)}, f32[8,128]{1,0:T(8,128)S(1)}, u32[]{:S(2)}, u32[]{:S(2)}) %collective-permute-start.5) | collective-permute-done | bytes 4128 | tf_op jit(solution)/shard_map/ppermute | solution.py:564
  29.3 0.1 clip.1.raw_cols
  29.4 1.5 %backward_outputs.1 = (bf16[128,2048]{1,0:T(8,128)(2,1)}, bf16[128,2048]{1,0:T(8,128)(2,1)}, f32[16,2048]{1,0:T(8,128)}, bf16[128,2048]{1,0:T(8,128)(2,1)}, bf16[128,2048]{1,0:T(8,128)(2,1)}) custom-call(bf16[128,2048]{1,0:T(8,128)(2,1)S(1)} %get-tuple-element.31.refs_0_.q_ref, bf16[128,2048]{1,0:T(8,128)(2,1)S(1)} %get-tuple-element.32.refs_1_.k_ref, ...), custom_call_target="tpu_custom_call" | custom-call | flops 4194304 | bytes 2097152 | tf_op jit(solution)/shard_map/backward_outputs/pallas_call | solution.py:601
  (8 shorter events, 0.0 us)
Async XLA Ops:
  7.0 1.6 %collective-permute-start = (f32[3,128,128]{2,1,0:T(8,128)S(1)}, f32[3,128,128]{2,1,0:T(8,128)S(1)}, u32[]{:S(2)}, u32[]{:S(2)}) collective-permute-start(f32[3,128,128]{2,1,0:T(8,128)S(1)} %get-tuple-element.38), channel_id=1, source_target_pairs={{0,4},{4,0},{8,12},{12,8},{16,20},{20,16},{24,28},{28,24},{1,5},{5... | collective-permute-start | bytes 589832 | tf_op jit(solution)/shard_map/ppermute | solution.py:470
  8.7 6.1 %collective-permute-start.1 = (bf16[3,128,128]{2,1,0:T(8,128)(2,1)S(1)}, bf16[3,128,128]{2,1,0:T(8,128)(2,1)S(1)}, u32[]{:S(2)}, u32[]{:S(2)}) collective-permute-start(bf16[3,128,128]{2,1,0:T(8,128)(2,1)S(1)} %get-tuple-element.40), channel_id=1, source_target_pairs={{0,8},{4,12},{8,0},{12,4},{16,24},{20,28},{24,16},{28,20},{1,9},{5... | collective-permute-start | bytes 294920 | tf_op jit(solution)/shard_map/ppermute | solution.py:470
  14.9 5.4 %collective-permute-start.2 = (bf16[2,128,128]{2,1,0:T(8,128)(2,1)S(1)}, bf16[2,128,128]{2,1,0:T(8,128)(2,1)S(1)}, u32[]{:S(2)}, u32[]{:S(2)}) collective-permute-start(bf16[2,128,128]{2,1,0:T(8,128)(2,1)S(1)} %get-tuple-element.44), channel_id=1, source_target_pairs={{0,16},{4,20},{8,24},{12,28},{16,0},{20,4},{24,8},{28,12},{1,17},{... | collective-permute-start | bytes 196616 | tf_op jit(solution)/shard_map/ppermute | solution.py:470
  20.5 1.5 %collective-permute-start.3 = (f32[392,128]{1,0:T(8,128)S(1)}, f32[392,128]{1,0:T(8,128)S(1)}, u32[]{:S(2)}, u32[]{:S(2)}) collective-permute-start(f32[392,128]{1,0:T(8,128)S(1)} %get-tuple-element.47), channel_id=1, source_target_pairs={{0,4},{4,0},{8,12},{12,8},{16,20},{20,16},{24,28},{28,24},{1,5},{5... | collective-permute-start | bytes 602120 | tf_op jit(solution)/shard_map/ppermute | solution.py:470
  22.0 1.6 %copy-start = (f32[2048]{0:T(1024)S(1)}, f32[2048]{0:T(1024)}, u32[]{:S(2)}) copy-start(f32[2048]{0:T(1024)} %param.12) | copy-start | bytes 24580
  22.0 3.7 %collective-permute-start.4 = (f32[8,128]{1,0:T(8,128)S(1)}, f32[8,128]{1,0:T(8,128)S(1)}, u32[]{:S(2)}, u32[]{:S(2)}) collective-permute-start(f32[8,128]{1,0:T(8,128)S(1)} %square_sum.2.refs_9_.left_ref), channel_id=1, source_target_pairs={{0,1},{1,0},{2,3},{3,2},{4,5},{5,4},{6,7},{7,6},{8,9},{9,8},{10,11... | collective-permute-start | bytes 12296 | tf_op jit(solution)/shard_map/ppermute | solution.py:564
  25.7 3.6 %collective-permute-start.5 = (f32[8,128]{1,0:T(8,128)S(1)}, f32[8,128]{1,0:T(8,128)S(1)}, u32[]{:S(2)}, u32[]{:S(2)}) collective-permute-start(f32[8,128]{1,0:T(8,128)S(1)} %square_sum.3.refs_4_.refs_1_), channel_id=1, source_target_pairs={{0,2},{1,3},{2,0},{3,1},{4,6},{5,7},{6,4},{7,5},{8,10},{9,11},{10,... | collective-permute-start | bytes 12296 | tf_op jit(solution)/shard_map/ppermute | solution.py:564
where the time goes:
time: 31.1 us; the launch traced here: 30.9 us
  Pallas kernels  16.1 us (52%)
  starting transfers between devices  9.48 us (30%)
  waiting for transfers between devices  4.59 us (15%)
  between operations  0.71 us (2%)
    ppermute x4, starting transfers between devices, swap(): return lax.ppermute(value, 'ctx', [(i, i ^ 1 << bit) for i in range(ctx)])  6.41 us
    pallas_call x1, Pallas kernels, shards(): pl.pallas_call(states_kernel, in_specs=[HBM] * 6, out_specs=[VMEM] * 10,...  6.39 us
    pallas_call x3, Pallas kernels, local(): pl.pallas_call(partial(local_kernel, reverse, which, modes), out_shape=[r...  4.66 us
    ppermute x4, waiting for transfers between devices, swap(): return lax.ppermute(value, 'ctx', [(i, i ^ 1 << bit) for i in range(ctx)])  3.53 us
    ppermute x2, starting transfers between devices, tp_swap(): return lax.ppermute(value, 'tp', [(i, i ^ 1 << bit) for i in range(tp)])  3.07 us
    pallas_call x1, Pallas kernels, shards(): pl.pallas_call(partial(forward_kernel, modes, blocks), out_shape=[line_sh...  1.84 us
    pallas_call x1, Pallas kernels, shards(): pl.pallas_call(backward_kernel, in_specs=[VMEM] * 9, out_specs=[HBM] * 5,...  1.5 us
    pallas_call x1, Pallas kernels, shards(): pl.pallas_call(partial(adjoint_kernel, modes, blocks), out_shape=whole, s...  1.29 us
  transfers between devices with their start and end apart: 6, of which 6 were waited for; matrix products, arithmetic and copies ran while one was open for 0% of the time, Pallas kernels for 25%

commit v1 on v0

--- a/solution.py
+++ b/solution.py
@@ -38,14 +38,78 @@
     return items[0]
 
 
-def states_kernel(
+def half_units(which, blocks, modes, sub):
+    if blocks == 1:
+        return [(0, which * (modes // 2 * sub), modes // 2)]
+    count = blocks // 2
+    return [
+        (which * count + j, (which * count + j) * (modes * sub), modes) for j in range(count)
+    ]
+
+
+def to_scan_order(to_scan, left, right, part, i, block, target):
+    size, sub = to_scan.shape[0], to_scan.shape[0] // part
+    rows = slice(i * part, (i + 1) * part)
+    stacked = []
+    for s in range(sub):
+        cols = pl.ds(pl.multiple_of((block * sub + s) * LANES, LANES), LANES)
+        product = left[rows, cols].astype(F32) * right[rows, cols].astype(F32)
+        stacked.append(product.astype(jnp.bfloat16))
+    target[block, i * size : (i + 1) * size, :] = jnp.dot(
+        to_scan, jnp.concatenate(stacked, axis=0), preferred_element_type=F32
+    )
+
+
+def scan_states(unit, sub, part, gated_ref, pulled_ref, rate_ref, before_part, out_ref, at_row):
+    block, base, modes = unit
+    seq = gated_ref.shape[1] // sub
+    decay = [
+        jnp.exp(-rate_ref[pl.ds(pl.multiple_of(base + n * sub, sub), sub), :])
+        for n in range(modes)
+    ]
+    first = tuple(jnp.zeros((sub, LANES), F32) for _ in range(modes))
+    carry = (first, first)
+    for i in range(seq // part):
+        before_part(i)
+
+        def forward(j, carry):
+            held, inner = list(carry[0]), list(carry[1])
+            for u in range(UNROLL):
+                at = pl.ds(pl.multiple_of((i * part + j * UNROLL + u) * sub, sub), sub)
+                x = gated_ref[block, at, :]
+                p = pulled_ref[block, at, :]
+                for n in range(modes):
+                    held[n] = decay[n] * held[n] + x
+                    inner[n] = inner[n] + p * held[n]
+            return tuple(held), tuple(inner)
+
+        carry = lax.fori_loop(0, part // UNROLL, forward, carry)
+
+    def backward(j, carry):
+        held = list(carry)
+        for u in range(UNROLL):
+            at = pl.ds(pl.multiple_of((seq - 1 - (j * UNROLL + u)) * sub, sub), sub)
+            p = pulled_ref[block, at, :]
+            for n in range(modes):
+                held[n] = decay[n] * held[n] + p
+        return tuple(held)
+
+    for n in range(modes):
+        rows = slice(at_row + n * sub, at_row + (n + 1) * sub)
+        out_ref[0, rows, :] = carry[0][n]
+        out_ref[2, rows, :] = carry[1][n]
+    starts = lax.fori_loop(0, seq // UNROLL, backward, first)
+    for n in range(modes):
+        out_ref[1, at_row + n * sub : at_row + (n + 1) * sub, :] = starts[n]
+
+
+def send_kernel(
     q_hbm,
     k_hbm,
     v_hbm,
     ct_hbm,
     rate_hbm,
     res_hbm,
-    keep_ref,
     send_ref,
     q_ref,
     k_ref,
@@ -57,7 +121,6 @@
     coef_ref,
     rate_cols,
     res_cols,
-    states,
     sems,
 ):
     seq, channels = q_ref.shape
@@ -66,105 +129,98 @@
     sub = channels // (blocks * LANES)
     part = math.gcd(seq, STEP_ROWS)
     parts = seq // part
-    tables = [
-        pltpu.make_async_copy(rate_hbm, rate_cols, sems.at[4 * parts]),
-        pltpu.make_async_copy(res_hbm, res_cols, sems.at[4 * parts + 1]),
-    ]
-    lines = []
+    which = 1 - lax.axis_index("ctx") % 2
+    pairs = ((k_hbm, k_ref), (v_hbm, v_ref), (ct_hbm, ct_ref), (q_hbm, q_ref))
+    copies = []
+
+    def start(source, target):
+        copy = pltpu.make_async_copy(source, target, sems.at[len(copies)])
+        copy.start()
+        copies.append(copy)
+
+    start(rate_hbm, rate_cols)
+    width = channels // min(blocks, 2)
+    cols = pl.ds(pl.multiple_of(which * width, LANES) if blocks > 1 else 0, width)
     for i in range(parts):
         rows = pl.ds(i * part, part)
-        pairs = ((k_hbm, k_ref), (v_hbm, v_ref), (ct_hbm, ct_ref), (q_hbm, q_ref))
-        for j, (source, target) in enumerate(pairs):
-            lines.append(
-                pltpu.make_async_copy(source.at[rows], target.at[rows], sems.at[4 * i + j])
-            )
-    for copy in tables + lines:
+        for source, target in pairs:
+            start(source.at[rows, cols], target.at[rows, cols])
+    start(res_hbm, res_cols)
+    if blocks > 1:
+        cols = pl.ds(pl.multiple_of((1 - which) * width, LANES), width)
+        for source, target in pairs:
+            start(source.at[:, cols], target.at[:, cols])
+
+    def spread(source, target):
+        for b in range(blocks):
+            for s in range(sub):
+                cols = slice((b * sub + s) * LANES, (b * sub + s + 1) * LANES)
+                target[pl.ds(b * modes * sub + s, modes, stride=sub), :] = source[:, cols]
+
+    to_scan = reorder(part * sub, part, False)
+    copies[0].wait()
+    spread(rate_cols, rate_ref)
+    units = half_units(which, blocks, modes, sub)
+    for at, unit in enumerate(units):
+
+        def before_part(i):
+            if at == 0:
+                for copy in copies[1 + 4 * i : 5 + 4 * i]:
+                    copy.wait()
+            to_scan_order(to_scan, k_ref, v_ref, part, i, unit[0], gated_ref)
+            to_scan_order(to_scan, ct_ref, q_ref, part, i, unit[0], pulled_ref)
+
+        at_row = at * unit[2] * sub
+        scan_states(
+            unit, sub, part, gated_ref, pulled_ref, rate_ref, before_part, send_ref, at_row
+        )
+    for copy in copies[1 + 4 * parts :]:
+        copy.wait()
+    spread(res_cols, coef_ref)
+    coef_ref[...] = coef_ref[...] * jnp.sqrt(1.0 - jnp.exp(-2.0 * rate_ref[...]))
+
+
+def keep_kernel(
+    q_ref,
+    k_ref,
+    v_ref,
+    ct_ref,
+    rate_ref,
+    gated_in,
+    pulled_in,
+    keep_ref,
+    gated_ref,
+    pulled_ref,
+    sems,
+):
+    seq, channels = q_ref.shape
+    blocks = gated_ref.shape[0]
+    sub = channels // (blocks * LANES)
+    modes = rate_ref.shape[0] // (blocks * sub)
+    part = math.gcd(seq, STEP_ROWS)
+    to_scan = reorder(part * sub, part, False)
+    which = lax.axis_index("ctx") % 2
+    count = max(blocks // 2, 1)
+    done = pl.ds((1 - which) * count if blocks > 1 else 0, count)
+    copies = [
+        pltpu.make_async_copy(gated_in.at[done], gated_ref.at[done], sems.at[0]),
+        pltpu.make_async_copy(pulled_in.at[done], pulled_ref.at[done], sems.at[1]),
+    ]
+    for copy in copies:
         copy.start()
-    for copy in tables:
+    lines = (gated_ref, pulled_ref) if blocks > 1 else (gated_in, pulled_in)
+    units = half_units(which, blocks, modes, sub)
+    for at, unit in enumerate(units):
+
+        def before_part(i):
+            if blocks > 1:
+                to_scan_order(to_scan, k_ref, v_ref, part, i, unit[0], gated_ref)
+                to_scan_order(to_scan, ct_ref, q_ref, part, i, unit[0], pulled_ref)
+
+        at_row = at * unit[2] * sub
+        scan_states(unit, sub, part, *lines, rate_ref, before_part, keep_ref, at_row)
+    for copy in copies:
         copy.wait()
-    for b in range(blocks):
-        for s in range(sub):
-            cols = slice((b * sub + s) * LANES, (b * sub + s + 1) * LANES)
-            rows = pl.ds(b * modes * sub + s, modes, stride=sub)
-            rate_ref[rows, :] = rate_cols[:, cols]
-            coef_ref[rows, :] = res_cols[:, cols]
-    rate = rate_ref[...]
-    coef_ref[...] = coef_ref[...] * jnp.sqrt(1.0 - jnp.exp(-2.0 * rate))
-    to_scan = reorder(part * sub, part, False)
-
-    def to_scan_order(left, right, i, target):
-        rows = slice(i * part, (i + 1) * part)
-        product = (left[rows, :].astype(F32) * right[rows, :].astype(F32)).astype(jnp.bfloat16)
-        stacked = jnp.concatenate(
-            [
-                jnp.concatenate(
-                    [
-                        product[:, (b * sub + s) * LANES : (b * sub + s + 1) * LANES]
-                        for s in range(sub)
-                    ],
-                    axis=0,
-                )
-                for b in range(blocks)
-            ],
-            axis=1,
-        )
-        ordered = jnp.dot(to_scan, stacked, preferred_element_type=F32)
-        for b in range(blocks):
-            target[b, i * part * sub : (i + 1) * part * sub, :] = ordered[
-                :, b * LANES : (b + 1) * LANES
-            ]
-
-    mode_rows_of = partial(mode_rows, modes=modes, sub=sub)
-    for i in range(parts):
-        for copy in lines[4 * i : 4 * i + 4]:
-            copy.wait()
-        to_scan_order(k_ref, v_ref, i, gated_ref)
-        to_scan_order(ct_ref, q_ref, i, pulled_ref)
-        for b in range(blocks):
-            decay = [jnp.exp(-rate_ref[r, :]) for r in mode_rows_of(b)]
-
-            def forward(j, carry):
-                held, inner = list(carry[0]), list(carry[1])
-                for u in range(UNROLL):
-                    at = pl.ds(pl.multiple_of((i * part + j * UNROLL + u) * sub, sub), sub)
-                    x = gated_ref[b, at, :]
-                    p = pulled_ref[b, at, :]
-                    for n in range(modes):
-                        held[n] = decay[n] * held[n] + x
-                        inner[n] = inner[n] + p * held[n]
-                return tuple(held), tuple(inner)
-
-            if i == 0:
-                first = tuple(jnp.zeros((sub, LANES), F32) for _ in range(modes))
-                carry = (first, first)
-            else:
-                carry = tuple(tuple(states[kind, r, :] for r in mode_rows_of(b)) for kind in (0, 2))
-            ends, inner = lax.fori_loop(0, part // UNROLL, forward, carry)
-            for n, r in enumerate(mode_rows_of(b)):
-                states[0, r, :] = ends[n]
-                states[2, r, :] = inner[n]
-
-    for b in range(blocks):
-        decay = [jnp.exp(-rate_ref[r, :]) for r in mode_rows_of(b)]
-
-        def backward(j, carry):
-            held = list(carry)
-            for u in range(UNROLL):
-                at = pl.ds(pl.multiple_of((seq - 1 - (j * UNROLL + u)) * sub, sub), sub)
-                p = pulled_ref[b, at, :]
-                for n in range(modes):
-                    held[n] = decay[n] * held[n] + p
-            return tuple(held)
-
-        first = tuple(jnp.zeros((sub, LANES), F32) for _ in range(modes))
-        starts = lax.fori_loop(0, seq // UNROLL, backward, first)
-        for n, r in enumerate(mode_rows_of(b)):
-            states[1, r, :] = starts[n]
-
-    half = keep_ref.shape[1]
-    core = lax.axis_index("ctx") % 2
-    keep_ref[...] = states[:, pl.ds(pl.multiple_of(core * half, half), half), :]
-    send_ref[...] = states[:, pl.ds(pl.multiple_of((1 - core) * half, half), half), :]
 
 
 def own_rows(rate_ref, half):
@@ -347,14 +403,15 @@
         lax.fori_loop(0, seq // UNROLL, body, first)
 
 
-def line_outputs(left, right, scales, skip_ref, scanned, targets, done_with):
+def line_outputs(left, right, scales, skip_ref, scanned, targets, which, done_with=None):
     seq, channels = left.shape
     blocks = scanned.shape[0]
     sub = channels // (blocks * LANES)
     part = math.gcd(seq, STEP_ROWS)
     from_scan = reorder(part * sub, part, True)
-    for i in range(seq // part):
+    for i in which:
         rows = slice(i * part, (i + 1) * part)
+        to_rows = slice((i - which[0]) * part, (i - which[0] + 1) * part)
         stacked = jnp.concatenate(
             [scanned[b, i * part * sub : (i + 1) * part * sub, :] for b in range(blocks)], axis=1
         ).astype(jnp.bfloat16)
@@ -366,10 +423,11 @@
                 line = left[rows, cols].astype(F32) * right[rows, cols].astype(F32)
                 mixed = own + skip_ref[:, cols] * line.astype(jnp.bfloat16).astype(F32)
                 for scale, target in zip(scales, targets):
-                    target[rows, cols] = (scale[rows, cols].astype(F32) * mixed).astype(
+                    target[to_rows, cols] = (scale[rows, cols].astype(F32) * mixed).astype(
                         jnp.bfloat16
                     )
-        done_with(i, pl.ds(i * part, part))
+        if done_with is not None:
+            done_with(pl.ds((i - which[0]) * part, part), pl.ds(i * part, part))
 
 
 def forward_kernel(modes, blocks, *refs):
@@ -386,37 +444,46 @@
         skip_ref,
         scanned,
         (out_ref, gq_ref),
-        lambda i, at: None,
-    )
+        range(k_ref.shape[0] // math.gcd(k_ref.shape[0], STEP_ROWS)),
+    )
+
+
+def early_parts(seq):
+    parts = seq // math.gcd(seq, STEP_ROWS)
+    return range((parts + 1) // 2), range((parts + 1) // 2, parts)
 
 
 def adjoint_kernel(modes, blocks, *refs):
-    rate_ref, coef_ref, mine_ref, other_ref, _ = refs[:5]
-    local_refs = refs[5 : 5 + blocks]
-    scanned, states = refs[5 + blocks :]
+    q_ref, k_ref, v_ref, ct_ref, rate_ref, coef_ref, skip_ref, mine_ref, other_ref, _ = refs[:10]
+    local_refs, refs = refs[10 : 10 + blocks], refs[10 + blocks :]
+    out_rows, gq_rows, out_hbm, gq_hbm, scanned, gk_ref, gv_ref, states, sems = refs
+    copies = [
+        pltpu.make_async_copy(out_rows, out_hbm, sems.at[0]),
+        pltpu.make_async_copy(gq_rows, gq_hbm, sems.at[1]),
+    ]
+    for copy in copies:
+        copy.start()
     place_halves(mine_ref, other_ref, states.shape[0] // 2, states)
     add_carries(True, modes, rate_ref, coef_ref, states, local_refs, scanned)
-
-
-def backward_kernel(
-    q_ref,
-    k_ref,
-    v_ref,
-    ct_ref,
-    scanned,
-    skip_ref,
-    out_rows,
-    gq_rows,
-    raw_cols,
-    out_hbm,
-    gq_hbm,
-    raw_hbm,
-    gk_hbm,
-    gv_hbm,
-    gk_rows,
-    gv_rows,
-    sems,
-):
+    line_outputs(
+        ct_ref,
+        q_ref,
+        (v_ref, k_ref),
+        skip_ref,
+        scanned,
+        (gk_ref, gv_ref),
+        early_parts(q_ref.shape[0])[0],
+    )
+    for copy in copies:
+        copy.wait()
+
+
+def last_outputs_kernel(limit, *refs):
+    q_ref, k_ref, v_ref, ct_ref, scanned, skip_ref, gk_early, gv_early, mine_ref, other_ref = refs[
+        :10
+    ]
+    share_refs = refs[10:-8]
+    raw_hbm, gk_hbm, gv_hbm, gk_rows, gv_rows, raw_cols, states, sems = refs[-8:]
     copies = []
 
     def start(source, target):
@@ -424,13 +491,21 @@
         copy.start()
         copies.append(copy)
 
-    def send(i, at):
-        for source, target in ((gk_rows, gk_hbm), (gv_rows, gv_hbm)):
-            start(source.at[at], target.at[at])
-
-    for source, target in ((out_rows, out_hbm), (gq_rows, gq_hbm), (raw_cols, raw_hbm)):
-        start(source, target)
-    line_outputs(ct_ref, q_ref, (v_ref, k_ref), skip_ref, scanned, (gk_rows, gv_rows), send)
+    early = pl.ds(0, gk_early.shape[0])
+    start(gk_early, gk_hbm.at[early])
+    start(gv_early, gv_hbm.at[early])
+    clip(limit, scanned.shape[0], mine_ref, other_ref, share_refs, raw_cols, states)
+    start(raw_cols, raw_hbm)
+
+    def send(at, to):
+        start(gk_rows.at[at], gk_hbm.at[to])
+        start(gv_rows.at[at], gv_hbm.at[to])
+
+    late = early_parts(q_ref.shape[0])[1]
+    if len(late) > 0:
+        line_outputs(
+            ct_ref, q_ref, (v_ref, k_ref), skip_ref, scanned, (gk_rows, gv_rows), late, send
+        )
     for copy in copies:
         copy.wait()
 
@@ -439,8 +514,7 @@
     out_ref[...] = left_ref[...] + right_ref[...]
 
 
-def clip_kernel(limit, blocks, mine_ref, other_ref, *refs):
-    share_refs, (out_ref, states) = refs[1:-2], refs[-2:]
+def clip(limit, blocks, mine_ref, other_ref, share_refs, out_ref, states):
     modes = out_ref.shape[0]
     sub = out_ref.shape[1] // (blocks * LANES)
     half = states.shape[0] // 2
@@ -479,27 +553,36 @@
     elements = seq * channels * modes
     sources = (queries, keys_in, values_in, cotangent, decay_rates.T, residues.T)
 
-    keep, send, q, k, v, ct, gated, pulled, row_rates, row_coefs = pl.pallas_call(
-        states_kernel,
+    send, q, k, v, ct, gated, pulled, row_rates, row_coefs = pl.pallas_call(
+        send_kernel,
         in_specs=[HBM] * 6,
-        out_specs=[VMEM] * 10,
-        out_shape=[rows(3, half)] * 2
+        out_specs=[VMEM] * 9,
+        out_shape=[rows(3, half)]
         + [line_shape] * 4
         + [rows(blocks, seq * sub)] * 2
         + [rows(2 * half)] * 2,
         scratch_shapes=[
             table_scratch,
             table_scratch,
-            pltpu.VMEM((3, 2 * half, LANES), F32),
-            pltpu.SemaphoreType.DMA((4 * parts + 2,)),
+            pltpu.SemaphoreType.DMA((4 * parts + 6,)),
         ],
         compiler_params=KERNEL,
         cost_estimate=pl.CostEstimate(
-            flops=6 * elements, bytes_accessed=8 * seq * channels, transcendentals=0
+            flops=3 * elements, bytes_accessed=8 * seq * channels, transcendentals=0
         ),
-        name="chunk_states",
+        name="sent_states",
     )(*[pltpu.with_memory_space_constraint(item, pltpu.HBM) for item in sources])
     sibling = swap(send, 0)
+    keep, gated, pulled = pl.pallas_call(
+        keep_kernel,
+        out_shape=[rows(3, half)] + [rows(blocks, seq * sub)] * 2,
+        scratch_shapes=[pltpu.SemaphoreType.DMA((2,))],
+        compiler_params=KERNEL,
+        cost_estimate=pl.CostEstimate(
+            flops=3 * elements, bytes_accessed=8 * seq * channels, transcendentals=0
+        ),
+        name="kept_states",
+    )(q, k, v, ct, row_rates, gated, pulled)
 
     def wire(level):
         return rows(2 if level == levels - 1 else 3, half, dtype=WIRE)
@@ -581,35 +664,53 @@
         square = plus(square, share, after)
         share = tp_swap(square, bit)
         after = square
-    scanned = pl.pallas_call(
+    early, late = early_parts(seq)
+    early_shape = jax.ShapeDtypeStruct((seq * len(early) // parts, channels), jnp.bfloat16)
+    late_scratch = pltpu.VMEM((seq * max(len(late), 1) // parts, channels), jnp.bfloat16)
+    operator_out, grad_queries, scanned, early_keys, early_values = pl.pallas_call(
         partial(adjoint_kernel, modes, blocks),
-        out_shape=whole,
-        scratch_shapes=[states_scratch],
+        in_specs=[VMEM] * (12 + blocks),
+        out_specs=[HBM] * 2 + [VMEM] * 3,
+        out_shape=[line_shape] * 2 + [whole] + [early_shape] * 2,
+        scratch_shapes=[states_scratch, pltpu.SemaphoreType.DMA((2,))],
         compiler_params=KERNEL,
         cost_estimate=pl.CostEstimate(
             flops=2 * elements, bytes_accessed=8 * seq * channels, transcendentals=0
         ),
         name="adjoint_carries",
-    )(row_rates, row_coefs, mine, other, after, *adj)
-    clipped = pl.pallas_call(
-        partial(clip_kernel, math.sqrt(channels * tp * modes), blocks),
-        out_shape=table_shape,
-        scratch_shapes=[states_scratch],
-        compiler_params=KERNEL,
-        name="clip",
-    )(mine, other, scanned, square, share)
-    operator_out, grad_queries, grad_residues, grad_keys, grad_values = pl.pallas_call(
-        backward_kernel,
-        in_specs=[VMEM] * 9,
-        out_specs=[HBM] * 5,
-        out_shape=[line_shape] * 2 + [table_shape] + [line_shape] * 2,
-        scratch_shapes=[line_scratch] * 2 + [pltpu.SemaphoreType.DMA((2 * parts + 3,))],
+    )(
+        q,
+        k,
+        v,
+        ct,
+        row_rates,
+        row_coefs,
+        skip,
+        mine,
+        other,
+        after,
+        *adj,
+        forward_out,
+        forward_grad,
+    )
+    grad_residues, grad_keys, grad_values = pl.pallas_call(
+        partial(last_outputs_kernel, math.sqrt(channels * tp * modes)),
+        in_specs=[VMEM] * 12,
+        out_specs=[HBM] * 3,
+        out_shape=[table_shape] + [line_shape] * 2,
+        scratch_shapes=[
+            late_scratch,
+            late_scratch,
+            table_scratch,
+            states_scratch,
+            pltpu.SemaphoreType.DMA((2 * parts + 3,)),
+        ],
         compiler_params=KERNEL,
         cost_estimate=pl.CostEstimate(
             flops=elements, bytes_accessed=8 * seq * channels, transcendentals=0
         ),
-        name="backward_outputs",
-    )(q, k, v, ct, scanned, skip, forward_out, forward_grad, clipped)
+        name="last_outputs",
+    )(q, k, v, ct, scanned, skip, early_keys, early_values, mine, other, square, share)
     return (operator_out, grad_queries, grad_keys, grad_values, grad_residues.T)
 
 

time: 31.1 us -> 31.7 us (1.019)
  Pallas kernels: 16.1 us -> 17.1 us
  starting transfers between devices: 9.48 us -> 9.14 us
    pallas_call x4, Pallas kernels: 9.31 us -> 10.2 us  [the longest x1 4.27 us: shards(): pl.pallas_call(send_kernel, in_specs=[HBM] * 6, out_specs=[VMEM] * 9, out...]
    ppermute x4, waiting for transfers between devices: 3.53 us -> 3.92 us  [swap(): return lax.ppermute(value, 'ctx', [(i, i ^ 1 << bit) for i in range(ctx)])]
    ppermute x2, waiting for transfers between devices: 1.06 us -> 0.67 us  [tp_swap(): return lax.ppermute(value, 'tp', [(i, i ^ 1 << bit) for i in range(tp)])]
    ppermute x4, starting transfers between devices: 6.41 us -> 6.07 us  [swap(): return lax.ppermute(value, 'ctx', [(i, i ^ 1 << bit) for i in range(ctx)])]
  transfers between devices with their start and end apart: 6 -> 6, of which waited for: 6 -> 5; matrix products, arithmetic and copies ran while one was open for 0% -> 0% of each run, Pallas kernels for 25% -> 35%
where the time goes in v1:
time: 31.7 us; the launch traced here: 31.6 us
  Pallas kernels  17.1 us (54%)
  starting transfers between devices  9.14 us (29%)
  waiting for transfers between devices  4.6 us (15%)
  between operations  0.73 us (2%)
    ppermute x4, starting transfers between devices, swap(): return lax.ppermute(value, 'ctx', [(i, i ^ 1 << bit) for i in range(ctx)])  6.07 us
    pallas_call x3, Pallas kernels, local(): pl.pallas_call(partial(local_kernel, reverse, which, modes), out_shape=[r...  4.65 us
    pallas_call x1, Pallas kernels, shards(): pl.pallas_call(send_kernel, in_specs=[HBM] * 6, out_specs=[VMEM] * 9, out...  4.27 us
    ppermute x4, waiting for transfers between devices, swap(): return lax.ppermute(value, 'ctx', [(i, i ^ 1 << bit) for i in range(ctx)])  3.92 us
    ppermute x2, starting transfers between devices, tp_swap(): return lax.ppermute(value, 'tp', [(i, i ^ 1 << bit) for i in range(tp)])  3.07 us
    pallas_call x1, Pallas kernels, shards(): pl.pallas_call(keep_kernel, out_shape=[rows(3, half)] + [rows(blocks, seq...  3.04 us
    pallas_call x1, Pallas kernels, shards(): pl.pallas_call(partial(forward_kernel, modes, blocks), out_shape=[line_sh...  1.88 us
    pallas_call x1, Pallas kernels, shards(): pl.pallas_call(partial(adjoint_kernel, modes, blocks), in_specs=[VMEM] *...  1.64 us
  transfers between devices with their start and end apart: 6, of which 5 were waited for; matrix products, arithmetic and copies ran while one was open for 0% of the time, Pallas kernels for 35%

profile of v1, /device:TPU:0, one launch (start us, length us, event | category | flops | bytes accessed | tf_op | source)
XLA Modules:
  0.0 31.6 jit_solution(1177901538097111555)
XLA Ops:
  0.6 4.3 %sent_states.1 = (f32[3,128,128]{2,1,0:T(8,128)S(1)}, bf16[128,2048]{1,0:T(8,128)(2,1)S(1)}, bf16[128,2048]{1,0:T(8,128)(2,1)S(1)}, bf16[128,2048]{1,0:T(8,128)(...) custom-call(bf16[128,2048]{1,0:T(8,128)(2,1)} %q_hbm.1, ...), custom_call_target="tpu_custom_call" | custom-call | flops 12582912 | bytes 2097152 | tf_op jit(solution)/shard_map/sent_states/pallas_call | solution.py:556
  4.9 0.5 %collective-permute-start = (f32[3,128,128]{2,1,0:T(8,128)S(1)}, f32[3,128,128]{2,1,0:T(8,128)S(1)}, u32[]{:S(2)}, u32[]{:S(2)}) collective-permute-start(f32[3,128,128]{2,1,0:T(8,128)S(1)} %get-tuple-element.45), channel_id=1, source_target_pairs={{0,4},{4,0},{8,12},{12,8},{16,20},{20,16},{24,28},{28,24},{1,5},{5... | collective-permute-start | bytes 589832 | tf_op jit(solution)/shard_map/ppermute | solution.py:544
  5.4 3.0 %kept_states.1 = (f32[3,128,128]{2,1,0:T(8,128)S(1)}, f32[2,1024,128]{2,1,0:T(8,128)S(1)}, f32[2,1024,128]{2,1,0:T(8,128)S(1)}) custom-call(bf16[128,2048]{1,0:T(8,128)(2,1)S(1)} %get-tuple-element.36.q_ref.refs_0_, bf16[128,2048]{1,0:T(8,128)(2,1)S(1)} %get-tuple-element.37.k_ref.refs_1_, bf16[128,2048]{1,0:T(8,128)(2,1)S(1)} %get-tuple-element.38.v_ref.refs_2_, ...), custom_call_target="tpu_custom_call" | custom-call | flops 12582912 | bytes 2097152 | tf_op jit(solution)/shard_map/kept_states/pallas_call | solution.py:576
  8.5 0.0 collective-permute-done.got_ref.sibling_ref
  8.5 0.1 chip_states.1
  8.6 2.7 %collective-permute-start.1 = (bf16[3,128,128]{2,1,0:T(8,128)(2,1)S(1)}, bf16[3,128,128]{2,1,0:T(8,128)(2,1)S(1)}, u32[]{:S(2)}, u32[]{:S(2)}) collective-permute-start(bf16[3,128,128]{2,1,0:T(8,128)(2,1)S(1)} %get-tuple-element.47), channel_id=1, source_target_pairs={{0,8},{4,12},{8,0},{12,4},{16,24},{20,28},{24,16},{28,20},{1,9},{5... | collective-permute-start | bytes 294920 | tf_op jit(solution)/shard_map/ppermute | solution.py:544
  11.2 2.3 %local_conv.1 = (f32[1024,128]{1,0:T(8,128)S(1)}, f32[1024,128]{1,0:T(8,128)S(1)}) custom-call(f32[2,1024,128]{2,1,0:T(8,128)S(1)} %get-tuple-element.48.lines_ref, f32[256,128]{1,0:T(8,128)S(1)} %get-tuple-element.40.rate_ref.refs_4_, f32[256,128]{1,0:T(8,128)S(1)} %get-tuple-element.41.coef_ref.refs_5_, f32[8,128]{1,0:T(8,128)S(1)} %slice_bitcast_fusion.1.after_ref), custom_call_target="tpu_custom_call" | custom-call | flops 16777216 | bytes 2097152 | tf_op jit(solution)/shard_map/local_conv/pallas_call | solution.py:597
  13.6 1.1 %collective-permute-done.1.got_ref = bf16[3,128,128]{2,1,0:T(8,128)(2,1)S(1)} collective-permute-done((bf16[3,128,128]{2,1,0:T(8,128)(2,1)S(1)}, bf16[3,128,128]{2,1,0:T(8,128)(2,1)S(1)}, u32[]{:S(2)}, u32[]{:S(2)}) %collective-permute-start.1) | collective-permute-done | bytes 98336 | tf_op jit(solution)/shard_map/ppermute | solution.py:544
  14.7 0.1 block_states.1
  14.8 2.8 %collective-permute-start.2 = (bf16[2,128,128]{2,1,0:T(8,128)(2,1)S(1)}, bf16[2,128,128]{2,1,0:T(8,128)(2,1)S(1)}, u32[]{:S(2)}, u32[]{:S(2)}) collective-permute-start(bf16[2,128,128]{2,1,0:T(8,128)(2,1)S(1)} %get-tuple-element.51), channel_id=1, source_target_pairs={{0,16},{4,20},{8,24},{12,28},{16,0},{20,4},{24,8},{28,12},{1,17},{... | collective-permute-start | bytes 196616 | tf_op jit(solution)/shard_map/ppermute | solution.py:544
  17.6 1.2 %local_adjoint.1.after_ref.refs_10_ = f32[1024,128]{1,0:T(8,128)S(1)} custom-call(f32[2,1024,128]{2,1,0:T(8,128)S(1)} %get-tuple-element.52.lines_ref, f32[256,128]{1,0:T(8,128)S(1)} %get-tuple-element.40.rate_ref.refs_4_, f32[256,128]{1,0:T(8,128)S(1)} %get-tuple-element.41.coef_ref.refs_5_, f32[8,128]{1,0:T(8,128)S(1)} %slice_bitcast_fusion.after_ref), custom_call_target="tpu_custom_call" | custom-call | flops 16777216 | bytes 2097152 | tf_op jit(solution)/shard_map/local_adjoint/pallas_call | solution.py:597
  18.8 2.6 %collective-permute-done.2.got_ref = bf16[2,128,128]{2,1,0:T(8,128)(2,1)S(1)} collective-permute-done((bf16[2,128,128]{2,1,0:T(8,128)(2,1)S(1)}, bf16[2,128,128]{2,1,0:T(8,128)(2,1)S(1)}, u32[]{:S(2)}, u32[]{:S(2)}) %collective-permute-start.2) | collective-permute-done | bytes 65568 | tf_op jit(solution)/shard_map/ppermute | solution.py:544
  21.3 0.1 carries.1
  21.5 0.1 collective-permute-start.3
  21.6 1.2 %late_adjoint.1.after_ref.refs_11_ = f32[1024,128]{1,0:T(8,128)S(1)} custom-call(f32[2,1024,128]{2,1,0:T(8,128)S(1)} %get-tuple-element.52.lines_ref, f32[256,128]{1,0:T(8,128)S(1)} %get-tuple-element.40.rate_ref.refs_4_, f32[256,128]{1,0:T(8,128)S(1)} %get-tuple-element.41.coef_ref.refs_5_, f32[8,128]{1,0:T(8,128)S(1)} %get-tuple-element.67.after_ref), custom_call_target="tpu_custom_call" | custom-call | flops 16777216 | bytes 2097152 | tf_op jit(solution)/shard_map/late_adjoint/pallas_call | solution.py:597
  22.7 0.2 collective-permute-done.3.refs_8_.refs_9_
  23.0 1.5 %collective-permute-start.4 = (f32[8,128]{1,0:T(8,128)S(1)}, f32[8,128]{1,0:T(8,128)S(1)}, u32[]{:S(2)}, u32[]{:S(2)}) collective-permute-start(f32[8,128]{1,0:T(8,128)S(1)} %square_sum.2.refs_9_.left_ref), channel_id=1, source_target_pairs={{0,1},{1,0},{2,3},{3,2},{4,5},{5,4},{6,7},{7,6},{8,9},{9,8},{10,11... | collective-permute-start | bytes 12296 | tf_op jit(solution)/shard_map/ppermute | solution.py:647
  24.5 0.0 copy-done
  24.5 1.9 %forward_outputs.1 = (bf16[128,2048]{1,0:T(8,128)(2,1)S(1)}, bf16[128,2048]{1,0:T(8,128)(2,1)S(1)}, f32[8,128]{1,0:T(8,128)S(1)}) custom-call(bf16[128,2048]{1,0:T(8,128)(2,1)S(1)} %get-tuple-element.36.q_ref.refs_0_, bf16[128,2048]{1,0:T(8,128)(2,1)S(1)} %get-tuple-element.37.k_ref.refs_1_, bf16[128,2048]{1,0:T(8,128)(2,1)S(1)} %get-tuple-element.38.v_ref.refs_2_, ...), custom_call_target="tpu_custom_call" | custom-call | flops 8388608 | bytes 4194304 | tf_op jit(solution)/shard_map/forward_outputs/pallas_call | solution.py:653
  26.4 0.2 collective-permute-done.4.right_ref
  26.7 1.5 %collective-permute-start.5 = (f32[8,128]{1,0:T(8,128)S(1)}, f32[8,128]{1,0:T(8,128)S(1)}, u32[]{:S(2)}, u32[]{:S(2)}) collective-permute-start(f32[8,128]{1,0:T(8,128)S(1)} %square_sum.3.refs_9_.refs_10_), channel_id=1, source_target_pairs={{0,2},{1,3},{2,0},{3,1},{4,6},{5,7},{6,4},{7,5},{8,10},{9,11},{10,... | collective-permute-start | bytes 12296 | tf_op jit(solution)/shard_map/ppermute | solution.py:647
  28.2 1.6 %adjoint_carries.1 = (bf16[128,2048]{1,0:T(8,128)(2,1)}, bf16[128,2048]{1,0:T(8,128)(2,1)}, f32[2,1024,128]{2,1,0:T(8,128)S(1)}, bf16[64,2048]{1,0:T(8,128)(2,1)S(1)}, bf16[64,2048]{1,0:T(8,128)(2,1)S(1)}) custom-call(bf16[128,2048]{1,0:T(8,128)(2,1)S(1)} %get-tuple-element.36.q_ref.refs_0_, bf16[128,2048]{1,0:T(8,128)(2,1)S(1)} %get-tuple-element.37.k_ref.refs_1_, ...), custom_call_target="tpu_custom_call" | custom-call | flops 8388608 | bytes 2097152 | tf_op jit(solution)/shard_map/adjoint_carries/pallas_call | solution.py:670
  29.8 0.4 %collective-permute-done.5.refs_11_ = f32[8,128]{1,0:T(8,128)S(1)} collective-permute-done((f32[8,128]{1,0:T(8,128)S(1)}, f32[8,128]{1,0:T(8,128)S(1)}, u32[]{:S(2)}, u32[]{:S(2)}) %collective-permute-start.5) | collective-permute-done | bytes 4128 | tf_op jit(solution)/shard_map/ppermute | solution.py:647
  30.3 1.3 %last_outputs.1 = (f32[16,2048]{1,0:T(8,128)}, bf16[128,2048]{1,0:T(8,128)(2,1)}, bf16[128,2048]{1,0:T(8,128)(2,1)}) custom-call(bf16[128,2048]{1,0:T(8,128)(2,1)S(1)} %get-tuple-element.36.q_ref.refs_0_, bf16[128,2048]{1,0:T(8,128)(2,1)S(1)} %get-tuple-element.37.k_ref.refs_1_, bf16[128,2048]{1,0:T(8,128)(2,1)S(1)} %get-tuple-element.38.v_ref.refs_2_, ...), custom_call_target="tpu_custom_call" | custom-call | flops 4194304 | bytes 2097152 | tf_op jit(solution)/shard_map/last_outputs/pallas_call | solution.py:696
  (8 shorter events, 0.0 us)
Async XLA Ops:
  4.9 3.6 %collective-permute-start = (f32[3,128,128]{2,1,0:T(8,128)S(1)}, f32[3,128,128]{2,1,0:T(8,128)S(1)}, u32[]{:S(2)}, u32[]{:S(2)}) collective-permute-start(f32[3,128,128]{2,1,0:T(8,128)S(1)} %get-tuple-element.45), channel_id=1, source_target_pairs={{0,4},{4,0},{8,12},{12,8},{16,20},{20,16},{24,28},{28,24},{1,5},{5... | collective-permute-start | bytes 589832 | tf_op jit(solution)/shard_map/ppermute | solution.py:544
  8.6 6.1 %collective-permute-start.1 = (bf16[3,128,128]{2,1,0:T(8,128)(2,1)S(1)}, bf16[3,128,128]{2,1,0:T(8,128)(2,1)S(1)}, u32[]{:S(2)}, u32[]{:S(2)}) collective-permute-start(bf16[3,128,128]{2,1,0:T(8,128)(2,1)S(1)} %get-tuple-element.47), channel_id=1, source_target_pairs={{0,8},{4,12},{8,0},{12,4},{16,24},{20,28},{24,16},{28,20},{1,9},{5... | collective-permute-start | bytes 294920 | tf_op jit(solution)/shard_map/ppermute | solution.py:544
  14.8 6.5 %collective-permute-start.2 = (bf16[2,128,128]{2,1,0:T(8,128)(2,1)S(1)}, bf16[2,128,128]{2,1,0:T(8,128)(2,1)S(1)}, u32[]{:S(2)}, u32[]{:S(2)}) collective-permute-start(bf16[2,128,128]{2,1,0:T(8,128)(2,1)S(1)} %get-tuple-element.51), channel_id=1, source_target_pairs={{0,16},{4,20},{8,24},{12,28},{16,0},{20,4},{24,8},{28,12},{1,17},{... | collective-permute-start | bytes 196616 | tf_op jit(solution)/shard_map/ppermute | solution.py:544
  21.5 1.5 %collective-permute-start.3 = (f32[392,128]{1,0:T(8,128)S(1)}, f32[392,128]{1,0:T(8,128)S(1)}, u32[]{:S(2)}, u32[]{:S(2)}) collective-permute-start(f32[392,128]{1,0:T(8,128)S(1)} %get-tuple-element.54), channel_id=1, source_target_pairs={{0,4},{4,0},{8,12},{12,8},{16,20},{20,16},{24,28},{28,24},{1,5},{5... | collective-permute-start | bytes 602120 | tf_op jit(solution)/shard_map/ppermute | solution.py:544
  23.0 1.6 %copy-start = (f32[2048]{0:T(1024)S(1)}, f32[2048]{0:T(1024)}, u32[]{:S(2)}) copy-start(f32[2048]{0:T(1024)} %param.12) | copy-start | bytes 24580
  23.0 3.7 %collective-permute-start.4 = (f32[8,128]{1,0:T(8,128)S(1)}, f32[8,128]{1,0:T(8,128)S(1)}, u32[]{:S(2)}, u32[]{:S(2)}) collective-permute-start(f32[8,128]{1,0:T(8,128)S(1)} %square_sum.2.refs_9_.left_ref), channel_id=1, source_target_pairs={{0,1},{1,0},{2,3},{3,2},{4,5},{5,4},{6,7},{7,6},{8,9},{9,8},{10,11... | collective-permute-start | bytes 12296 | tf_op jit(solution)/shard_map/ppermute | solution.py:647
  26.7 3.6 %collective-permute-start.5 = (f32[8,128]{1,0:T(8,128)S(1)}, f32[8,128]{1,0:T(8,128)S(1)}, u32[]{:S(2)}, u32[]{:S(2)}) collective-permute-start(f32[8,128]{1,0:T(8,128)S(1)} %square_sum.3.refs_9_.refs_10_), channel_id=1, source_target_pairs={{0,2},{1,3},{2,0},{3,1},{4,6},{5,7},{6,4},{7,5},{8,10},{9,11},{10,... | collective-permute-start | bytes 12296 | tf_op jit(solution)/shard_map/ppermute | solution.py:647
